TPU v7x, 32 devices: a whole 2x2x4 slice. The times are simulated.
32 devices in a mesh: parts: 2 (over y), pool: 4 (over z), tp: 2 (over x), sub: 2 (over core).
Axes of the slice: x: 2, y: 2, z: 4, core: 2. Of those that a mesh axis runs over, the one named last changes fastest.
Arguments:
- deltas: bfloat16 [32, 2, 512, 1024], P(('parts', 'pool'), None, 'sub', 'tp'), parts along dimension 0, may hold values from -6 to 6
- anchors: bfloat16 [32, 2, 32, 1024], P(('parts', 'pool'), None, 'sub', 'tp'), parts along dimension 0, may hold values from -6 to 6
- chan_scale: bfloat16 [32, 2, 1024], P(('parts', 'pool'), None, 'tp'), parts along dimension 0, may hold values from 0.049804688 to 0.5
- lengths: int32 [32], P(('parts', 'pool')), parts along dimension 0, may hold values from 128 to 512, as said below
- route: int32 [32], P(('parts', 'pool')), parts along dimension 0, may hold values from 0 to 3, as said below
- new_query: bfloat16 [32, 4, 8192], P(('parts', 'pool'), None, ('tp', 'sub')), parts along dimension 0, may hold values from -32 to 32
- new_kv: bfloat16 [32, 2, 4, 1024], P(('parts', 'pool'), None, None, 'tp'), parts along dimension 0, may hold values from -8 to 8
Outputs:
- cache: bfloat16 [32, 2, 512, 1024], P(('parts', 'pool'), None, 'sub', 'tp'), parts along dimension 0
- attended: bfloat16 [32, 4, 8192], P(('parts', 'pool'), None, ('tp', 'sub')), parts along dimension 0
There are 2 independent parts, one for each index of `parts`. A program takes and returns all parts, laid end to end along the dimension named above; each array names one. Nothing has to cross between parts.
Inputs may be any that keep to these rules, and one draw needn't show every extreme that they name: `lengths`: multiples of 128; every draw holds a request of length 512. `route`: each prefill index sends exactly 1 of its requests to every decode group.
All inputs are finite; a program needn't handle non-finite values.
Results may differ from a plain program's by a relative error of at most 0.003.
Values may be sent and summed in bfloat16 or wider, within the bound.
No kernel may reach another device: no remote copies, remote signals or barrier semaphores. Data moves between devices by JAX's collectives and lax.ppermute only.
A program may use at most 64 MiB of HBM per device.

v0:
```python
import functools
import math

import jax
import jax.numpy as jnp
from jax import lax
from jax.experimental import pallas as pl
from jax.experimental.pallas import tpu as pltpu
from jax.sharding import PartitionSpec as P

HEAD_DIM = 128
Q_PER_KV = 8
TILE = 16
PAGE = 128
BF = jnp.bfloat16
F32 = jnp.float32
LOW = -1e30
NT = (((1,), (1,)), ((), ()))

IN_VMEM = pl.BlockSpec(memory_space=pltpu.VMEM)
IN_SMEM = pl.BlockSpec(memory_space=pltpu.SMEM)
IN_HBM = pl.BlockSpec(memory_space=pltpu.HBM)
LIMIT = pltpu.CompilerParams(vmem_limit_bytes=16 * 1024 * 1024)


def vmem(x):
    return pltpu.with_memory_space_constraint(x, pltpu.VMEM)


def hbm(x):
    return pltpu.with_memory_space_constraint(x, pltpu.HBM)


class Sizes:
    def __init__(self, deltas, anchors, new_query, n):
        self.n = n
        self.count, _, self.span, self.channels = deltas.shape
        self.rows = anchors.shape[2]
        self.repeat = self.span // self.rows
        self.steps = new_query.shape[1]
        self.heads = self.channels // HEAD_DIM
        self.q_local = new_query.shape[2] // HEAD_DIM
        self.mine = max(1, self.q_local // Q_PER_KV)
        self.rest = self.heads - self.mine
        self.group = self.q_local // self.mine
        self.wide = self.group * self.steps
        self.pages = self.span // PAGE
        self.page_rows = PAGE // self.repeat

    def anchor_at(self, which, parts):
        return (len(parts) * self.span + parts.index(which) * self.rows) * self.heads

    def side_at(self, parts):
        return len(parts) * self.heads * (self.span + self.rows)

    def message_rows(self, parts):
        return self.side_at(parts) + (TILE if 0 in parts else 0)

    def page_anchor_at(self):
        return 2 * self.heads * PAGE

    def page_side_at(self):
        return 2 * self.heads * (PAGE + self.page_rows)

    def page_message_rows(self, pages=1):
        return pages * (self.page_side_at() + TILE)

    def partner(self, k):
        return lax.axis_index("pool") ^ k


def request_for(size, k, route):
    index = jnp.int32(0)
    for j in range(size.count):
        index = jnp.where(route[j] == size.partner(k), jnp.int32(j), index)
    return index


def side_block(size, scale, length):
    row = lax.broadcasted_iota(jnp.int32, (TILE, HEAD_DIM), 0)
    scale = scale.astype(F32)
    out = jnp.where(row == 2 * size.heads, length.astype(F32), jnp.float32(0.0))
    for which in range(2):
        for h in range(size.heads):
            piece = scale[which:which + 1, h * HEAD_DIM:(h + 1) * HEAD_DIM]
            out = jnp.where(row == which * size.heads + h, piece, out)
    return out.astype(BF)


def pack_kernel(size, plan, more, route, lengths, deltas, anchors, scale, *rest):
    outs, (held, tables, block, sems) = rest[:-4], rest[-4:]
    sub = lax.axis_index("sub")
    work = []
    for slot, (low, high, kind) in enumerate(plan):
        index = request_for(size, jnp.where(sub == 0, low, high), route)
        copies = []
        for which in range(2):
            for source, target, s in ((deltas, held, 0), (anchors, tables, 1)):
                copy = pltpu.make_async_copy(
                    source.at[index, which], target.at[2 * slot + which], sems.at[s, 2 * slot + which]
                )
                copy.start()
                copies.append(copy)
        many = outputs_of(size, kind)
        work.append((2 * slot, kind, index, copies, outs[:many]))
        outs = outs[many:]
    for k, out in zip(more, outs):
        out[...] = jnp.full(out.shape, lengths[request_for(size, k, route)], jnp.int32)
    for slot, kind, index, copies, msgs in work:
        side = side_block(size, scale[index], lengths[index])
        for copy in copies:
            copy.wait()

        def fill_whole(msg, slot=slot, side=side):
            for which in range(2):
                for h in range(size.heads):
                    lanes = slice(h * HEAD_DIM, (h + 1) * HEAD_DIM)
                    at = (which * size.heads + h) * size.span
                    msg[at:at + size.span, :] = held[slot + which, :, lanes]
                    at = size.anchor_at(which, (0, 1)) + h * size.rows
                    msg[at:at + size.rows, :] = tables[slot + which, :, lanes]
            msg[size.side_at((0, 1)):size.side_at((0, 1)) + TILE, :] = side

        def fill_pages(slot=slot, side=side, msgs=msgs[1:]):
            for page in range(size.pages):
                base = page * size.page_message_rows()
                for which in range(2):
                    table = tables[slot + which].astype(F32)
                    for h in range(size.heads):
                        lanes = slice(h * HEAD_DIM, (h + 1) * HEAD_DIM)
                        at = base + (which * size.heads + h) * PAGE
                        for msg in msgs[page:]:
                            msg[at:at + PAGE, :] = held[slot + which, page * PAGE:(page + 1) * PAGE, lanes]
                        at = (which * size.heads + h) * size.page_rows
                        first = page * size.page_rows
                        block[at:at + size.page_rows, :] = table[first:first + size.page_rows, lanes]
                at, end = base + size.page_anchor_at(), base + size.page_side_at()
                for msg in msgs[page:]:
                    msg[at:end, :] = block[...].astype(BF)
                    msg[end:end + TILE, :] = side

        if kind == "own":
            fill_whole(msgs[0])
        else:
            pl.when(sub == 0)(functools.partial(fill_whole, msgs[0]))
            pl.when(sub != 0)(fill_pages if kind == "pages" else functools.partial(fill_whole, msgs[1]))


def outputs_of(size, kind):
    return {"own": 1, "front": 2, "pages": 1 + size.pages}[kind]


def pack(size, plan, more, route, lengths, deltas, anchors, scale):
    shapes = []
    for _, _, kind in plan:
        rows = [size.message_rows((0, 1))] * (1 if kind != "front" else 2)
        if kind == "pages":
            rows += [size.page_message_rows(p + 1) for p in range(size.pages)]
        shapes += [pltpu.VMEM((r, HEAD_DIM), BF) for r in rows]
    shapes += [pltpu.VMEM((8, HEAD_DIM), jnp.int32)] * len(more)
    slots = 2 * len(plan)
    outs = pl.pallas_call(
        functools.partial(pack_kernel, size, plan, more),
        out_shape=shapes,
        in_specs=[IN_SMEM, IN_SMEM, IN_HBM, IN_HBM, IN_VMEM],
        out_specs=[IN_VMEM] * len(shapes),
        scratch_shapes=[
            pltpu.VMEM((slots, size.span, size.channels), BF),
            pltpu.VMEM((slots, size.rows, size.channels), BF),
            pltpu.VMEM((2 * size.heads * size.page_rows, HEAD_DIM), F32),
            pltpu.SemaphoreType.DMA((2, slots)),
        ],
        compiler_params=LIMIT,
        cost_estimate=pl.CostEstimate(
            flops=0, bytes_accessed=2 * slots * size.span * size.channels, transcendentals=0
        ),
    )(hbm(route), hbm(lengths), hbm(deltas), hbm(anchors), hbm(scale))
    got = []
    for _, _, kind in plan:
        many = outputs_of(size, kind)
        got.append(outs[:many])
        outs = outs[many:]
    return got, outs


def levels_kernel(size, many, *refs):
    sub = lax.axis_index("sub")
    for sent, got, out in zip(refs[:many], refs[many:2 * many], refs[2 * many + 1:]):
        longer = jnp.max(jnp.maximum(sent[...], got[...]))
        pages = (longer + (PAGE - 1)) // PAGE - size.pages
        out[0] = jnp.where(sub == 0, 0, jnp.clip(pages, 0, size.pages))


def levels_of(size, sent, got, message):
    many = len(sent)
    out = pl.pallas_call(
        functools.partial(levels_kernel, size, many),
        in_specs=[IN_VMEM] * (2 * many + 1),
        out_specs=[IN_SMEM] * many + [IN_VMEM],
        out_shape=[jax.ShapeDtypeStruct((1,), jnp.int32)] * many + [pltpu.VMEM(message.shape, BF)],
        input_output_aliases={2 * many: many},
        compiler_params=LIMIT,
    )(*[vmem(x) for x in (*sent, *got, message)])
    return out[:many], out[many]


def arrange_kernel(size, new_query, new_kv, query, fresh, wide, tall):
    sub = lax.axis_index("sub")
    rest = size.heads - size.mine
    tall[...] = jnp.zeros_like(tall)
    for r in range(size.count):
        for j in range(size.mine):
            for g in range(size.group):
                at = (j * size.group + g) * HEAD_DIM
                piece = new_query[r, :, at:at + HEAD_DIM].astype(F32)
                wide[g * size.steps:(g + 1) * size.steps, :] = piece
            query[r, j] = wide[...].astype(BF)
            for which in range(2):
                own, other = (
                    new_kv[r, which, :, h * HEAD_DIM:(h + 1) * HEAD_DIM].astype(F32) for h in (j, j + rest)
                )
                tall[:size.steps, :] = jnp.where(sub == 0, own, other)
                fresh[r, which, j] = tall[...].astype(BF)


def arrange(size, new_query, new_kv):
    return pl.pallas_call(
        functools.partial(arrange_kernel, size),
        in_specs=[IN_VMEM, IN_VMEM],
        out_specs=[IN_VMEM, IN_VMEM],
        out_shape=[
            pltpu.VMEM((size.count, size.mine, size.wide, HEAD_DIM), BF),
            pltpu.VMEM((size.count, 2, size.mine, TILE, HEAD_DIM), BF),
        ],
        scratch_shapes=[pltpu.VMEM((size.wide, HEAD_DIM), F32), pltpu.VMEM((TILE, HEAD_DIM), F32)],
        compiler_params=LIMIT,
    )(hbm(new_query), hbm(new_kv))


def row_copies(size, k, parts, cache, mine, theirs, sems):
    sub = lax.axis_index("sub")
    row = size.partner(k)
    copies = []
    for o, (out, first) in enumerate(((mine, sub * size.rest), (theirs, (1 - sub) * size.rest))):
        if o and not size.rest:
            break
        for p, which in enumerate(parts):
            for j in range(size.mine):
                lanes = pl.ds(pl.multiple_of((first + j) * HEAD_DIM, HEAD_DIM), HEAD_DIM)
                at = (p * size.mine + j) * size.span
                copies.append(pltpu.make_async_copy(
                    out.at[pl.ds(at, size.span)],
                    cache.at[row, which, :, lanes],
                    sems.at[o, p * size.mine + j],
                ))
    return copies


def rebuild_kernel(size, paged, chained, gated, low, *refs):
    high, refs = refs[:1 + paged], refs[1 + paged:]
    mine, theirs, limit = refs[gated + 2 * chained + 2:][:3]
    sub = lax.axis_index("sub")

    def fill(upper):
        if upper and paged:
            pages, lens = high
            at = size.page_side_at()
            side = pages[at:at + TILE, :].astype(F32)
            bases = [p * size.page_message_rows() for p in range(size.pages)]
            blocks = [pages[x + size.page_anchor_at():x + at, :].astype(F32) for x in bases]
            length = lens[0:1, :].astype(F32)
        else:
            message = high[0] if upper else low
            at = size.side_at((0, 1))
            side = message[at:at + TILE, :].astype(F32)
            length = side[2 * size.heads:2 * size.heads + 1, :]
        limit[...] = jnp.broadcast_to(length, limit.shape)
        for o, out in enumerate((theirs, mine)):
            first = size.rest if (o == 0) != upper else 0
            for which in range(2):
                for j in range(size.mine):
                    h = which * size.heads + first + j
                    scale = side[h:h + 1, :]
                    to = (which * size.mine + j) * size.span
                    if not (upper and paged):
                        at = size.anchor_at(which, (0, 1)) + (first + j) * size.rows
                        table = message[at:at + size.rows, :].astype(F32)
                    for i in range(size.rows):
                        if upper and paged:
                            page, r = divmod(i, size.page_rows)
                            anchor = blocks[page][h * size.page_rows + r:h * size.page_rows + r + 1, :]
                            at = bases[page] + h * PAGE + r * size.repeat
                            delta = pages[at:at + size.repeat, :]
                        else:
                            anchor = table[i:i + 1, :]
                            at = h * size.span + i * size.repeat
                            delta = message[at:at + size.repeat, :]
                        value = anchor + scale * delta.astype(F32)
                        keep = float(int(upper) * size.span + i * size.repeat) < length
                        value = jnp.where(keep, value, jnp.float32(0.0)).astype(BF)
                        out[to + i * size.repeat:to + (i + 1) * size.repeat, :] = value

    pl.when(sub == 0)(functools.partial(fill, False))
    pl.when(sub != 0)(functools.partial(fill, True))


def rebuild(size, low, high, gate, state):
    args = [vmem(x) for x in (low, *high, *gate)]
    in_specs = [IN_VMEM] * len(args)
    aliases = {len(args) - 1: 5} if gate else {}
    if state is not None:
        aliases |= {len(args): 0, len(args) + 1: 1}
        args += list(state)
        in_specs += [IN_HBM, IN_HBM]
    given = (2 * size.mine * size.span, HEAD_DIM)
    out = pl.pallas_call(
        functools.partial(rebuild_kernel, size, len(high) > 1, state is not None, len(gate)),
        in_specs=in_specs,
        out_specs=[IN_HBM, IN_HBM, IN_VMEM, IN_VMEM, IN_VMEM] + [IN_VMEM] * len(gate),
        out_shape=[
            pltpu.HBM((size.count, 2, size.span, size.channels), BF),
            pltpu.HBM((size.count, size.steps, size.q_local * HEAD_DIM), BF),
            pltpu.VMEM(given, BF),
            pltpu.VMEM(given, BF),
            pltpu.VMEM((8, HEAD_DIM), F32),
        ] + [pltpu.VMEM(x.shape, BF) for x in gate],
        input_output_aliases=aliases,
        compiler_params=LIMIT,
        cost_estimate=pl.CostEstimate(
            flops=8 * size.span * size.channels,
            bytes_accessed=12 * size.span * size.channels,
            transcendentals=0,
        ),
    )(*args)
    return tuple(out[:2]), out[2:5], out[5:]


def weigh(size, j, q, new_key, key_mine, key_other, live_mine, live_other, causal):
    factor = 1.0 / math.sqrt(HEAD_DIM)
    s0 = lax.dot_general(q, key_mine, NT, preferred_element_type=F32) * factor
    s1 = lax.dot_general(q, key_other, NT, preferred_element_type=F32) * factor
    s2 = lax.dot_general(q, new_key, NT, preferred_element_type=F32) * factor
    s0 = jnp.where(live_mine, s0, jnp.float32(LOW))
    s1 = jnp.where(live_other, s1, jnp.float32(LOW))
    s2 = jnp.where(causal, s2, jnp.float32(LOW))
    top = jnp.maximum(
        jnp.max(jnp.maximum(s0, s1), axis=1, keepdims=True), jnp.max(s2, axis=1, keepdims=True)
    )
    w0 = jnp.where(live_mine, jnp.exp(s0 - top), jnp.float32(0.0))
    w1 = jnp.where(live_other, jnp.exp(s1 - top), jnp.float32(0.0))
    w2 = jnp.where(causal, jnp.exp(s2 - top), jnp.float32(0.0))
    total = jnp.sum(w0 + w1, axis=1, keepdims=True) + jnp.sum(w2, axis=1, keepdims=True)
    return w0.astype(BF), w1.astype(BF), w2.astype(BF), total


def masks(size, length, fresh):
    sub = lax.axis_index("sub")
    limit = length[0:1, 0:1]
    spot = lax.broadcasted_iota(jnp.int32, (1, size.span), 1)
    live_mine = (spot + sub * size.span).astype(F32) < limit
    live_other = (spot + (1 - sub) * size.span).astype(F32) < limit
    step = lax.broadcasted_iota(jnp.int32, (size.wide, fresh), 0) % size.steps
    token = lax.broadcasted_iota(jnp.int32, (size.wide, fresh), 1)
    return live_mine, live_other, (token <= step) & (token < size.steps)


def start_store(size, k, parts, cache, mine, theirs, sems):
    copies = row_copies(size, k, parts, cache, mine, theirs, sems)
    for copy in copies:
        copy.start()
    return copies


def store_heads(size, k, flat, made, attended, sem, copies):
    for j in range(size.mine):
        for g in range(size.group):
            at = (j * size.group + g) * HEAD_DIM
            made[:, at:at + HEAD_DIM] = flat[j, g * size.steps:(g + 1) * size.steps, :].astype(BF)
    copy = pltpu.make_async_copy(made, attended.at[size.partner(k)], sem)
    copy.start()
    for each in copies:
        each.wait()
    copy.wait()


def attend_kernel(size, k, after, gated, query, new_kv, length, mine, other, theirs, *refs):
    refs = refs[after + gated + 2:]
    cache, attended, (made, flat, sem, sems) = refs[0], refs[1], refs[-4:]
    row = size.partner(k)
    copies = start_store(size, k, (0, 1), cache, mine, theirs, sems)
    live_mine, live_other, causal = masks(size, length, new_kv.shape[3])
    for j in range(size.mine):
        keys = slice(j * size.span, (j + 1) * size.span)
        values = slice((size.mine + j) * size.span, (size.mine + j + 1) * size.span)
        w0, w1, w2, total = weigh(
            size, j, query[row, j], new_kv[row, 0, j], mine[keys, :], other[keys, :],
            live_mine, live_other, causal,
        )
        acc = jnp.dot(w0, mine[values, :], preferred_element_type=F32)
        acc = acc + jnp.dot(w1, other[values, :], preferred_element_type=F32)
        acc = acc + jnp.dot(w2, new_kv[row, 1, j], preferred_element_type=F32)
        flat[j] = acc / total
    store_heads(size, k, flat, made, attended, sem, copies)


def attend(size, k, query, fresh, length, mine, other, theirs, after, gate, state):
    args = [vmem(x) for x in (query, fresh, length, mine, other, theirs, *after, *gate)]
    in_specs = [IN_VMEM] * len(args) + [IN_HBM, IN_HBM]
    flops = 8 * size.mine * size.wide * size.span * HEAD_DIM
    aliases = {len(args): 0, len(args) + 1: 1} | ({len(args) - 1: 2} if gate else {})
    out = pl.pallas_call(
        functools.partial(attend_kernel, size, k, len(after), len(gate)),
        in_specs=in_specs,
        out_specs=[IN_HBM, IN_HBM] + [IN_VMEM] * len(gate),
        out_shape=[pltpu.HBM(x.shape, x.dtype) for x in state] + [pltpu.VMEM(x.shape, BF) for x in gate],
        scratch_shapes=[
            pltpu.VMEM((size.steps, size.q_local * HEAD_DIM), BF),
            pltpu.VMEM((size.mine, size.wide, HEAD_DIM), F32),
            pltpu.SemaphoreType.DMA,
            pltpu.SemaphoreType.DMA((2, 2 * size.mine)),
        ],
        input_output_aliases=aliases,
        compiler_params=LIMIT,
        cost_estimate=pl.CostEstimate(
            flops=flops,
            bytes_accessed=8 * size.span * size.channels,
            transcendentals=2 * size.mine * size.wide * size.span,
        ),
    )(*args, *state)
    return tuple(out[:2]), out[2:]


def body(deltas, anchors, chan_scale, lengths, route, new_query, new_kv):
    n = lax.axis_size("pool")
    size = Sizes(deltas, anchors, new_query, n)
    raw = (route, lengths, deltas, anchors, chan_scale)
    others = list(range(2, n))
    lows = [1] + others[1:]

    def move(x, low=None, high=None):
        pairs = []
        for z in range(n):
            if low is not None:
                pairs.append((2 * z, 2 * (z ^ low)))
            if high is not None:
                pairs.append((2 * z + 1, 2 * (z ^ high) + 1))
        return lax.ppermute(x, ("pool", "sub"), pairs)

    def upper(level, pages, k):
        def branch(many):
            def send(*xs):
                if many == 0:
                    return xs[-1]
                x = move(xs[many - 1], high=k)
                return x if many == size.pages else jnp.concatenate([x, xs[-1][x.shape[0]:]])
            return send
        return lax.switch(level.reshape(()), [branch(many) for many in range(size.pages + 1)], *pages)

    def swapped(x):
        return lax.ppermute(x, "sub", [(0, 1), (1, 0)])

    [(front, near)], sent = pack(size, [(2, 1, "front")], others, *raw)
    whole = {2: move(front, low=2)}
    got = [move(x, high=k) for x, k in zip(sent, others)]
    levels, near = levels_of(size, sent, got, near)
    near = move(near, high=1)
    plan = [(low, k, "pages") for low, k in zip(lows, others)] + [(0, 0, "own")]
    mixed, _ = pack(size, plan, [], *raw)
    whole.update({low: move(x[0], low=low) for low, x in zip(lows, mixed)})
    paged = {k: list(x[1:]) for k, x in zip(others, mixed)}
    levels, arrived = dict(zip(others, levels)), dict(zip(others, got))
    query, fresh = arrange(size, new_query, new_kv)

    def gate_of(k):
        return [paged[k][-1]] if k in paged else []

    def opened(k, gate):
        if gate:
            paged[k][-1] = gate[0]

    held = []

    def take(k, high, following, state):
        gate = gate_of(following)
        state, (mine, theirs, length), gate = rebuild(size, whole[k], high, gate, state)
        opened(following, gate)
        held.append((k, query, fresh, length, mine, swapped(theirs), theirs))
        return state

    whole[0] = mixed[-1][0]
    state = take(0, [whole[0]], None, None)
    state, gate = attend(size, *held.pop(), (), gate_of(2), state)
    opened(2, gate)
    pages = upper(levels[2], paged[2], 2)
    state = take(2, [pages, arrived[2]], None, state)
    state = take(1, [near], 3, state)
    for k in others[1:]:
        pages = upper(levels[k], paged[k], k)
        for each in held:
            state, _ = attend(size, *each, [pages], (), state)
        held.clear()
        state = take(k, [pages, arrived[k]], k + 1, state)
    for each in held:
        state, _ = attend(size, *each, (), (), state)
    return state


def solution(mesh):
    placed = (
        P(("parts", "pool"), None, "sub", "tp"),
        P(("parts", "pool"), None, "sub", "tp"),
        P(("parts", "pool"), None, "tp"),
        P(("parts", "pool")),
        P(("parts", "pool")),
        P(("parts", "pool"), None, ("tp", "sub")),
        P(("parts", "pool"), None, None, "tp"),
    )
    return jax.shard_map(
        body,
        mesh=mesh,
        in_specs=placed,
        out_specs=(
            P(("parts", "pool"), None, "sub", "tp"),
            P(("parts", "pool"), None, ("tp", "sub")),
        ),
        check_vma=False,
    )
```

profile of v0, /device:TPU:0, one launch (start us, length us, event | category | flops | bytes accessed | tf_op | source)
XLA Modules:
  0.0 69.9 jit_solution(3910036961410904095)
XLA Ops:
  0.6 2.7 %shard_map.88 = (bf16[2192,128]{1,0:T(8,128)(2,1)}, bf16[2192,128]{1,0:T(8,128)(2,1)S(1)}, s32[8,128]{1,0:T(8,128)S(1)}, s32[8,128]{1,0:T(8,128)S(1)}) custom-call(s32[4]{0:T(128)} %route.3, s32[4]{0:T(128)} %lengths.3, bf16[4,2,256,512]{3,2,1,0:T(8,128)(2,1)} %deltas.3, bf16[4,2,16,512]{3,2,1,0:T(8,128)(2,1)} %anchors.3, bf16[4,2,512]{2,1,0:T(2,128)(2,1)} %scale.3), custom_call_target="tpu_custom_call" | custom-call | bytes 524288 | tf_op jit(solution)/shard_map/pallas_call | solution.py:162
  3.3 0.7 collective-permute-start.5
  4.0 0.7 collective-permute-start.6
  4.7 5.9 %collective-permute-start.9 = (bf16[2192,128]{1,0:T(8,128)(2,1)}, bf16[2192,128]{1,0:T(8,128)(2,1)S(1)}, u32[]{:S(2)}, u32[]{:S(2)}) collective-permute-start(bf16[2192,128]{1,0:T(8,128)(2,1)} %get-tuple-element.80), channel_id=1, source_target_pairs={{0,8},{4,12},{8,0},{12,4},{2,10},{6,14},{10,2},{14,6},{16,24},{20,... | collective-permute-start | bytes 1683464 | tf_op jit(solution)/shard_map/ppermute | solution.py:447
  10.6 3.3 %shard_map.87 = (bf16[2192,128]{1,0:T(8,128)(2,1)}, bf16[1104,128]{1,0:T(8,128)(2,1)S(1)}, bf16[2208,128]{1,0:T(8,128)(2,1)S(1)}, bf16[2192,128]{1,0:T(8,128)(2,...) custom-call(s32[4]{0:T(128)} %route.3, s32[4]{0:T(128)} %lengths.3, ...), custom_call_target="tpu_custom_call" | custom-call | bytes 1572864 | tf_op jit(solution)/shard_map/pallas_call | solution.py:162
  13.9 0.0 copy-start.4
  13.9 0.7 %copy-done.4 = bf16[1104,128]{1,0:T(8,128)(2,1)} copy-done((bf16[1104,128]{1,0:T(8,128)(2,1)}, bf16[1104,128]{1,0:T(8,128)(2,1)S(1)}, u32[]{:S(2)}) %copy-start.4) | copy-done | bytes 282648
  14.6 0.0 copy-start.2
  14.6 3.5 %collective-permute-start.7 = (bf16[2192,128]{1,0:T(8,128)(2,1)}, bf16[2192,128]{1,0:T(8,128)(2,1)S(1)}, u32[]{:S(2)}, u32[]{:S(2)}) collective-permute-start(bf16[2192,128]{1,0:T(8,128)(2,1)} %get-tuple-element.77), channel_id=1, source_target_pairs={{0,4},{4,0},{8,12},{12,8},{2,6},{6,2},{10,14},{14,10},{16,20},{20,... | collective-permute-start | bytes 1683464 | tf_op jit(solution)/shard_map/ppermute | solution.py:447
  18.1 0.0 collective-permute-done.5.refs_2_.refs_1_
  18.1 0.0 collective-permute-done.6.refs_3_.refs_1_
  18.1 0.7 %shard_map.89 = (s32[1]{0:T(128)}, s32[1]{0:T(128)}, bf16[2192,128]{1,0:T(8,128)(2,1)S(1)}) custom-call(s32[8,128]{1,0:T(8,128)S(1)} %get-tuple-element.73.refs_0_, s32[8,128]{1,0:T(8,128)S(1)} %get-tuple-element.74.refs_1_, s32[8,128]{1,0:T(8,128)S(1)} %collective-permute-done.5.refs_2_.refs_1_, ...), custom_call_target="tpu_custom_call", output_to_operand_aliasing={{2}: (4, {})} | custom-call | tf_op jit(solution)/shard_map/pallas_call | solution.py:196
  18.9 1.5 %collective-permute-start.8 = (bf16[2192,128]{1,0:T(8,128)(2,1)S(1)}, bf16[2192,128]{1,0:T(8,128)(2,1)}, u32[]{:S(2)}, u32[]{:S(2)}) collective-permute-start(bf16[2192,128]{1,0:T(8,128)(2,1)S(1)} %get-tuple-element.78), channel_id=1, source_target_pairs={{1,5},{5,1},{9,13},{13,9},{3,7},{7,3},{11,15},{15,11},{17,21},{21,... | collective-permute-start | bytes 1683464 | tf_op jit(solution)/shard_map/ppermute | solution.py:447
  20.3 1.9 %collective-permute-start.4 = (bf16[2192,128]{1,0:T(8,128)(2,1)}, bf16[2192,128]{1,0:T(8,128)(2,1)S(1)}, u32[]{:S(2)}, u32[]{:S(2)}) collective-permute-start(bf16[2192,128]{1,0:T(8,128)(2,1)} %get-tuple-element.72), channel_id=1, source_target_pairs={{0,12},{4,8},{8,4},{12,0},{2,14},{6,10},{10,6},{14,2},{16,28},{20,... | collective-permute-start | bytes 1683464 | tf_op jit(solution)/shard_map/ppermute | solution.py:447
  22.3 0.2 shard_map.90
  22.5 1.4 %collective-permute-start.10 = (bf16[1024,128]{1,0:T(8,128)(2,1)S(1)}, bf16[1024,128]{1,0:T(8,128)(2,1)S(1)}, u32[]{:S(2)}, u32[]{:S(2)}) collective-permute-start(bf16[1024,128]{1,0:T(8,128)(2,1)S(1)} %get-tuple-element.85.theirs), channel_id=1, source_target_pairs={{0,1},{1,0},{2,3},{3,2},{4,5},{5,4},{6,7},{7,6},{8,9},{9,8},{10,11... | collective-permute-start | bytes 786440 | tf_op jit(solution)/shard_map/ppermute | solution.py:460
  23.8 0.9 %shard_map.86 = (bf16[4,2,32,128]{3,2,1,0:T(8,128)(2,1)S(1)}, bf16[4,2,2,16,128]{4,3,2,1,0:T(8,128)(2,1)S(1)}) custom-call(bf16[4,4,2048]{2,1,0:T(4,128)(2,1)} %new_query.1, bf16[4,2,4,512]{3,2,1,0:T(4,128)(2,1)} %new_kv.1), custom_call_target="tpu_custom_call" | custom-call | tf_op jit(solution)/shard_map/pallas_call | solution.py:227
  25.4 0.0 collective-permute-done.10.other
  25.4 1.3 %shard_map.91 = (bf16[4,2,256,512]{3,2,1,0:T(8,128)(2,1)}, bf16[4,4,2048]{2,1,0:T(4,128)(2,1)}, bf16[2208,128]{1,0:T(8,128)(2,1)S(1)}) custom-call(bf16[4,2,32,128]{3,2,1,0:T(8,128)(2,1)S(1)} %get-tuple-element.70.query, bf16[4,2,2,16,128]{4,3,2,1,0:T(8,128)(2,1)S(1)} %get-tuple-element.71.new_kv, ...), custom_call_target="tpu_custom_call", output_to_operand_aliasing={{0}: (7, {}), {1}: (8, {}), {2}: (6, {})} | custom-call | flops 16777216 | bytes 1048576 | tf_op jit(solution)/shard_map/pallas_call | solution.py:411
  26.8 0.0 copy-done.2
  26.8 0.0 collective-permute-done.9.low
  26.8 0.9 %shard_map.92 = (bf16[4,2,256,512]{3,2,1,0:T(8,128)(2,1)}, bf16[4,4,2048]{2,1,0:T(4,128)(2,1)}, bf16[1024,128]{1,0:T(8,128)(2,1)S(1)}, bf16[1024,128]{1,0:T(8,128)(2,1)}, f32[8,128]{1,0:T(8,128)S(1)}) custom-call(bf16[2192,128]{1,0:T(8,128)(2,1)S(1)} %collective-permute-done.9.low, ...), custom_call_target="tpu_custom_call", output_to_operand_aliasing={{0}: (3, {}), {1}: (4, {})} | custom-call | flops 1048576 | bytes 1572864 | tf_op jit(solution)/shard_map/pallas_call | solution.py:316
  27.7 0.0 copy-start
  27.7 0.0 copy-start.3
  27.7 17.1 %collective-permute-start.12 = (bf16[1024,128]{1,0:T(8,128)(2,1)}, bf16[1024,128]{1,0:T(8,128)(2,1)S(1)}, u32[]{:S(2)}, u32[]{:S(2)}) collective-permute-start(bf16[1024,128]{1,0:T(8,128)(2,1)} %get-tuple-element.102.theirs), channel_id=1, source_target_pairs={{0,1},{1,0},{2,3},{3,2},{4,5},{5,4},{6,7},{7,6},{8,9},{9,8},{10,11... | collective-permute-start | bytes 786440 | tf_op jit(solution)/shard_map/ppermute | solution.py:460
  44.8 3.7 %collective-permute-done.7.low = bf16[2192,128]{1,0:T(8,128)(2,1)S(1)} collective-permute-done((bf16[2192,128]{1,0:T(8,128)(2,1)}, bf16[2192,128]{1,0:T(8,128)(2,1)S(1)}, u32[]{:S(2)}, u32[]{:S(2)}) %collective-permute-start.7) | collective-permute-done | bytes 561184 | tf_op jit(solution)/shard_map/ppermute | solution.py:447
  48.5 0.0 collective-permute-done.8.refs_0_
  48.5 1.2 %shard_map.93 = (bf16[4,2,256,512]{3,2,1,0:T(8,128)(2,1)}, bf16[4,4,2048]{2,1,0:T(4,128)(2,1)}, bf16[1024,128]{1,0:T(8,128)(2,1)S(1)}, bf16[1024,128]{1,0:T(8,12...) custom-call(bf16[2192,128]{1,0:T(8,128)(2,1)S(1)} %collective-permut, ...), custom_call_target="tpu_custom_call", output_to_operand_aliasing={{5}: (2, {}), {0}: (3, {}), {1}: (4, {})} | custom-call | flops 1048576 | bytes 1572864 | tf_op jit(solution)/shard_map/pallas_call | solution.py:316
  49.7 0.2 collective-permute-start.11
  50.6 0.0 copy-done
  50.6 0.0 copy-done.3
  50.6 0.0 copy-start.1
  50.6 0.0 collective-permute-done.12.other
  50.7 0.9 %copy-done.1 = bf16[1024,128]{1,0:T(8,128)(2,1)S(1)} copy-done((bf16[1024,128]{1,0:T(8,128)(2,1)S(1)}, bf16[1024,128]{1,0:T(8,128)(2,1)}, u32[]{:S(2)}) %copy-start.1) | copy-done | bytes 262168
  51.6 2.3 %shard_map.94 = (bf16[4,2,256,512]{3,2,1,0:T(8,128)(2,1)}, bf16[4,4,2048]{2,1,0:T(4,128)(2,1)}) custom-call(bf16[4,2,32,128]{3,2,1,0:T(8,128)(2,1)S(1)} %get-tuple-element.70.query, bf16[4,2,2,16,128]{4,3,2,1,0:T(8,128)(2,1)S(1)} %get-tuple-element.71.new_kv, f32[8,128]{1,0:T(8,128)S(1)} %get-tuple-element.100.length, ...), custom_call_target="tpu_custom_call", output_to_operand_aliasing={{0}: (7, {}), {1}: (8, {})} | custom-call | flops 16777216 | bytes 1048576 | tf_op jit(solution)/shard_map/pallas_call | solution.py:411
  53.9 0.0 collective-permute-done.11.other
  53.9 1.3 %shard_map.95 = (bf16[4,2,256,512]{3,2,1,0:T(8,128)(2,1)}, bf16[4,4,2048]{2,1,0:T(4,128)(2,1)}) custom-call(bf16[4,2,32,128]{3,2,1,0:T(8,128)(2,1)S(1)} %get-tuple-element.70.query, bf16[4,2,2,16,128]{4,3,2,1,0:T(8,128)(2,1)S(1)} %get-tuple-element.71.new_kv, f32[8,128]{1,0:T(8,128)S(1)} %get-tuple-element.97.length, ...), custom_call_target="tpu_custom_call", output_to_operand_aliasing={{0}: (7, {}), {1}: (8, {})} | custom-call | flops 16777216 | bytes 1048576 | tf_op jit(solution)/shard_map/pallas_call | solution.py:411
  55.2 0.0 collective-permute-done.4.low
  55.2 0.2 shard_map.96
  55.4 11.9 %collective-permute-start.13 = (bf16[1024,128]{1,0:T(8,128)(2,1)S(1)}, bf16[1024,128]{1,0:T(8,128)(2,1)S(1)}, u32[]{:S(2)}, u32[]{:S(2)}) collective-permute-start(bf16[1024,128]{1,0:T(8,128)(2,1)S(1)} %get-tuple-element.111.theirs), channel_id=1, source_target_pairs={{0,1},{1,0},{2,3},{3,2},{4,5},{5,4},{6,7},{7,6},{8,9},{9,8},{10,11... | collective-permute-start | bytes 786440 | tf_op jit(solution)/shard_map/ppermute | solution.py:460
  67.4 1.2 %collective-permute-done.13.other = bf16[1024,128]{1,0:T(8,128)(2,1)S(1)} collective-permute-done((bf16[1024,128]{1,0:T(8,128)(2,1)S(1)}, bf16[1024,128]{1,0:T(8,128)(2,1)S(1)}, u32[]{:S(2)}, u32[]{:S(2)}) %collective-permute-start.13) | collective-permute-done | bytes 262176 | tf_op jit(solution)/shard_map/ppermute | solution.py:460
  68.5 1.3 %shard_map.97 = (bf16[4,2,256,512]{3,2,1,0:T(8,128)(2,1)}, bf16[4,4,2048]{2,1,0:T(4,128)(2,1)}) custom-call(bf16[4,2,32,128]{3,2,1,0:T(8,128)(2,1)S(1)} %get-tuple-element.70.query, bf16[4,2,2,16,128]{4,3,2,1,0:T(8,128)(2,1)S(1)} %get-tuple-element.71.new_kv, f32[8,128]{1,0:T(8,128)S(1)} %get-tuple-element.109.length, ...), custom_call_target="tpu_custom_call", output_to_operand_aliasing={{0}: (6, {}), {1}: (7, {})} | custom-call | flops 16777216 | bytes 1048576 | tf_op jit(solution)/shard_map/pallas_call | solution.py:411
  (2 shorter events, 0.0 us)
Async XLA Ops:
  3.3 14.8 %collective-permute-start.5 = (s32[8,128]{1,0:T(8,128)S(1)}, s32[8,128]{1,0:T(8,128)S(1)}, u32[]{:S(2)}, u32[]{:S(2)}) collective-permute-start(s32[8,128]{1,0:T(8,128)S(1)} %get-tuple-element.73.refs_0_), channel_id=1, source_target_pairs={{1,9},{5,13},{9,1},{13,5},{3,11},{7,15},{11,3},{15,7},{17,25},{21,... | collective-permute-start | bytes 12296 | tf_op jit(solution)/shard_map/ppermute | solution.py:447
  4.0 14.1 %collective-permute-start.6 = (s32[8,128]{1,0:T(8,128)S(1)}, s32[8,128]{1,0:T(8,128)S(1)}, u32[]{:S(2)}, u32[]{:S(2)}) collective-permute-start(s32[8,128]{1,0:T(8,128)S(1)} %get-tuple-element.74.refs_1_), channel_id=1, source_target_pairs={{1,13},{5,9},{9,5},{13,1},{3,15},{7,11},{11,7},{15,3},{17,29},{21,... | collective-permute-start | bytes 12296 | tf_op jit(solution)/shard_map/ppermute | solution.py:447
  4.7 22.1 %collective-permute-start.9 = (bf16[2192,128]{1,0:T(8,128)(2,1)}, bf16[2192,128]{1,0:T(8,128)(2,1)S(1)}, u32[]{:S(2)}, u32[]{:S(2)}) collective-permute-start(bf16[2192,128]{1,0:T(8,128)(2,1)} %get-tuple-element.80), channel_id=1, source_target_pairs={{0,8},{4,12},{8,0},{12,4},{2,10},{6,14},{10,2},{14,6},{16,24},{20,... | collective-permute-start | bytes 1683464 | tf_op jit(solution)/shard_map/ppermute | solution.py:447
  13.9 0.7 %copy-start.4 = (bf16[1104,128]{1,0:T(8,128)(2,1)}, bf16[1104,128]{1,0:T(8,128)(2,1)S(1)}, u32[]{:S(2)}) copy-start(bf16[1104,128]{1,0:T(8,128)(2,1)S(1)} %get-tuple-element.90) | copy-start | bytes 847876
  14.6 12.2 %copy-start.2 = (bf16[1104,128]{1,0:T(8,128)(2,1)}, bf16[1104,128]{1,0:T(8,128)(2,1)S(1)}, u32[]{:S(2)}) copy-start(bf16[1104,128]{1,0:T(8,128)(2,1)S(1)} %get-tuple-element.96) | copy-start | bytes 847876
  14.6 33.9 %collective-permute-start.7 = (bf16[2192,128]{1,0:T(8,128)(2,1)}, bf16[2192,128]{1,0:T(8,128)(2,1)S(1)}, u32[]{:S(2)}, u32[]{:S(2)}) collective-permute-start(bf16[2192,128]{1,0:T(8,128)(2,1)} %get-tuple-element.77), channel_id=1, source_target_pairs={{0,4},{4,0},{8,12},{12,8},{2,6},{6,2},{10,14},{14,10},{16,20},{20,... | collective-permute-start | bytes 1683464 | tf_op jit(solution)/shard_map/ppermute | solution.py:447
  18.9 29.6 %collective-permute-start.8 = (bf16[2192,128]{1,0:T(8,128)(2,1)S(1)}, bf16[2192,128]{1,0:T(8,128)(2,1)}, u32[]{:S(2)}, u32[]{:S(2)}) collective-permute-start(bf16[2192,128]{1,0:T(8,128)(2,1)S(1)} %get-tuple-element.78), channel_id=1, source_target_pairs={{1,5},{5,1},{9,13},{13,9},{3,7},{7,3},{11,15},{15,11},{17,21},{21,... | collective-permute-start | bytes 1683464 | tf_op jit(solution)/shard_map/ppermute | solution.py:447
  20.3 34.9 %collective-permute-start.4 = (bf16[2192,128]{1,0:T(8,128)(2,1)}, bf16[2192,128]{1,0:T(8,128)(2,1)S(1)}, u32[]{:S(2)}, u32[]{:S(2)}) collective-permute-start(bf16[2192,128]{1,0:T(8,128)(2,1)} %get-tuple-element.72), channel_id=1, source_target_pairs={{0,12},{4,8},{8,4},{12,0},{2,14},{6,10},{10,6},{14,2},{16,28},{20,... | collective-permute-start | bytes 1683464 | tf_op jit(solution)/shard_map/ppermute | solution.py:447
  22.5 3.0 %collective-permute-start.10 = (bf16[1024,128]{1,0:T(8,128)(2,1)S(1)}, bf16[1024,128]{1,0:T(8,128)(2,1)S(1)}, u32[]{:S(2)}, u32[]{:S(2)}) collective-permute-start(bf16[1024,128]{1,0:T(8,128)(2,1)S(1)} %get-tuple-element.85.theirs), channel_id=1, source_target_pairs={{0,1},{1,0},{2,3},{3,2},{4,5},{5,4},{6,7},{7,6},{8,9},{9,8},{10,11... | collective-permute-start | bytes 786440 | tf_op jit(solution)/shard_map/ppermute | solution.py:460
  27.7 22.9 %copy-start = (bf16[1024,128]{1,0:T(8,128)(2,1)}, bf16[1024,128]{1,0:T(8,128)(2,1)S(1)}, u32[]{:S(2)}) copy-start(bf16[1024,128]{1,0:T(8,128)(2,1)S(1)} %get-tuple-element.101.mine) | copy-start | bytes 786436
  27.7 22.9 %copy-start.3 = (bf16[1104,128]{1,0:T(8,128)(2,1)S(1)}, bf16[1104,128]{1,0:T(8,128)(2,1)}, u32[]{:S(2)}) copy-start(bf16[1104,128]{1,0:T(8,128)(2,1)} %copy-done.2) | copy-start | bytes 847876
  27.7 22.9 %collective-permute-start.12 = (bf16[1024,128]{1,0:T(8,128)(2,1)}, bf16[1024,128]{1,0:T(8,128)(2,1)S(1)}, u32[]{:S(2)}, u32[]{:S(2)}) collective-permute-start(bf16[1024,128]{1,0:T(8,128)(2,1)} %get-tuple-element.102.theirs), channel_id=1, source_target_pairs={{0,1},{1,0},{2,3},{3,2},{4,5},{5,4},{6,7},{7,6},{8,9},{9,8},{10,11... | collective-permute-start | bytes 786440 | tf_op jit(solution)/shard_map/ppermute | solution.py:460
  49.7 4.1 %collective-permute-start.11 = (bf16[1024,128]{1,0:T(8,128)(2,1)S(1)}, bf16[1024,128]{1,0:T(8,128)(2,1)S(1)}, u32[]{:S(2)}, u32[]{:S(2)}) collective-permute-start(bf16[1024,128]{1,0:T(8,128)(2,1)S(1)} %get-tuple-element.99.theirs), channel_id=1, source_target_pairs={{0,1},{1,0},{2,3},{3,2},{4,5},{5,4},{6,7},{7,6},{8,9},{9,8},{10,11... | collective-permute-start | bytes 786440 | tf_op jit(solution)/shard_map/ppermute | solution.py:460
  50.6 1.0 %copy-start.1 = (bf16[1024,128]{1,0:T(8,128)(2,1)S(1)}, bf16[1024,128]{1,0:T(8,128)(2,1)}, u32[]{:S(2)}) copy-start(bf16[1024,128]{1,0:T(8,128)(2,1)} %copy-done) | copy-start | bytes 786436
  55.4 13.1 %collective-permute-start.13 = (bf16[1024,128]{1,0:T(8,128)(2,1)S(1)}, bf16[1024,128]{1,0:T(8,128)(2,1)S(1)}, u32[]{:S(2)}, u32[]{:S(2)}) collective-permute-start(bf16[1024,128]{1,0:T(8,128)(2,1)S(1)} %get-tuple-element.111.theirs), channel_id=1, source_target_pairs={{0,1},{1,0},{2,3},{3,2},{4,5},{5,4},{6,7},{7,6},{8,9},{9,8},{10,11... | collective-permute-start | bytes 786440 | tf_op jit(solution)/shard_map/ppermute | solution.py:460
where the time goes:
time: 70.1 us; the launch traced here: 69.9 us
  starting transfers between devices  44.7 us (64%)
  Pallas kernels  16.5 us (24%)
  waiting for transfers between devices  4.87 us (7%)
  between operations  2.2 us (3%)
  local copies, waits for them, and re-layouts  1.64 us (2%)
    ppermute x4, starting transfers between devices, swapped(): return lax.ppermute(x, 'sub', [(0, 1), (1, 0)])  30.5 us
    ppermute x6, starting transfers between devices, move(): return lax.ppermute(x, ('pool', 'sub'), pairs)  14.1 us
    pallas_call x4, Pallas kernels, attend(): pl.pallas_call(functools.partial(attend_kernel, size, k, len(after), len(...  6.3 us
    pallas_call x2, Pallas kernels, pack(): pl.pallas_call(functools.partial(pack_kernel, size, plan, more), out_shap...  5.96 us
    ppermute x6, waiting for transfers between devices, move(): return lax.ppermute(x, ('pool', 'sub'), pairs)  3.7 us
    pallas_call x4, Pallas kernels, rebuild(): pl.pallas_call(functools.partial(rebuild_kernel, size, len(high) > 1, sta...  2.53 us
    unnamed x10, local copies, waits for them, and re-layouts  1.64 us
  transfers between devices with their start and end apart: 10, of which 2 were waited for; matrix products, arithmetic and copies ran while one was open for 0% of the time, Pallas kernels for 17%

commit v1 on v0

--- a/solution.py
+++ b/solution.py
@@ -139,21 +139,21 @@
                     msg[at:end, :] = block[...].astype(BF)
                     msg[end:end + TILE, :] = side
 
-        if kind == "own":
+        if kind == "pages":
+            pl.when(sub == 0)(functools.partial(fill_whole, msgs[0]))
+            pl.when(sub != 0)(fill_pages)
+        else:
             fill_whole(msgs[0])
-        else:
-            pl.when(sub == 0)(functools.partial(fill_whole, msgs[0]))
-            pl.when(sub != 0)(fill_pages if kind == "pages" else functools.partial(fill_whole, msgs[1]))
 
 
 def outputs_of(size, kind):
-    return {"own": 1, "front": 2, "pages": 1 + size.pages}[kind]
+    return 1 + size.pages if kind == "pages" else 1
 
 
 def pack(size, plan, more, route, lengths, deltas, anchors, scale):
     shapes = []
     for _, _, kind in plan:
-        rows = [size.message_rows((0, 1))] * (1 if kind != "front" else 2)
+        rows = [size.message_rows((0, 1))]
         if kind == "pages":
             rows += [size.page_message_rows(p + 1) for p in range(size.pages)]
         shapes += [pltpu.VMEM((r, HEAD_DIM), BF) for r in rows]
@@ -175,6 +175,7 @@
             flops=0, bytes_accessed=2 * slots * size.span * size.channels, transcendentals=0
         ),
     )(hbm(route), hbm(lengths), hbm(deltas), hbm(anchors), hbm(scale))
+    outs = outs if isinstance(outs, (list, tuple)) else [outs]
     got = []
     for _, _, kind in plan:
         many = outputs_of(size, kind)
@@ -191,17 +192,15 @@
         out[0] = jnp.where(sub == 0, 0, jnp.clip(pages, 0, size.pages))
 
 
-def levels_of(size, sent, got, message):
+def levels_of(size, sent, got, after):
     many = len(sent)
-    out = pl.pallas_call(
+    return pl.pallas_call(
         functools.partial(levels_kernel, size, many),
         in_specs=[IN_VMEM] * (2 * many + 1),
-        out_specs=[IN_SMEM] * many + [IN_VMEM],
-        out_shape=[jax.ShapeDtypeStruct((1,), jnp.int32)] * many + [pltpu.VMEM(message.shape, BF)],
-        input_output_aliases={2 * many: many},
+        out_specs=[IN_SMEM] * many,
+        out_shape=[jax.ShapeDtypeStruct((1,), jnp.int32)] * many,
         compiler_params=LIMIT,
-    )(*[vmem(x) for x in (*sent, *got, message)])
-    return out[:many], out[many]
+    )(*[vmem(x) for x in (*sent, *got, after)])
 
 
 def arrange_kernel(size, new_query, new_kv, query, fresh, wide, tall):
@@ -459,17 +458,16 @@
     def swapped(x):
         return lax.ppermute(x, "sub", [(0, 1), (1, 0)])
 
-    [(front, near)], sent = pack(size, [(2, 1, "front")], others, *raw)
-    whole = {2: move(front, low=2)}
+    [(front,)], _ = pack(size, [(2, 1, "whole")], [], *raw)
+    plan = [(low, k, "pages") for low, k in zip(lows, others)] + [(0, 0, "whole")]
+    mixed, sent = pack(size, plan, others, *raw)
+    front = move(front, 2, 1)
     got = [move(x, high=k) for x, k in zip(sent, others)]
-    levels, near = levels_of(size, sent, got, near)
-    near = move(near, high=1)
-    plan = [(low, k, "pages") for low, k in zip(lows, others)] + [(0, 0, "own")]
-    mixed, _ = pack(size, plan, [], *raw)
-    whole.update({low: move(x[0], low=low) for low, x in zip(lows, mixed)})
+    whole = {low: move(x[0], low=low) for low, x in zip(lows, mixed)}
+    whole.update({2: front, 0: mixed[-1][0]})
     paged = {k: list(x[1:]) for k, x in zip(others, mixed)}
-    levels, arrived = dict(zip(others, levels)), dict(zip(others, got))
     query, fresh = arrange(size, new_query, new_kv)
+    levels, arrived = dict(zip(others, levels_of(size, sent, got, fresh))), dict(zip(others, got))
 
     def gate_of(k):
         return [paged[k][-1]] if k in paged else []
@@ -487,16 +485,13 @@
         held.append((k, query, fresh, length, mine, swapped(theirs), theirs))
         return state
 
-    whole[0] = mixed[-1][0]
-    state = take(0, [whole[0]], None, None)
-    state, gate = attend(size, *held.pop(), (), gate_of(2), state)
-    opened(2, gate)
     pages = upper(levels[2], paged[2], 2)
-    state = take(2, [pages, arrived[2]], None, state)
-    state = take(1, [near], 3, state)
+    state = take(2, [pages, arrived[2]], None, None)
+    state = take(1, [front], None, state)
+    state = take(0, [whole[0]], 3, state)
     for k in others[1:]:
         pages = upper(levels[k], paged[k], k)
-        for each in held:
+        for each in held[::-1]:
             state, _ = attend(size, *each, [pages], (), state)
         held.clear()
         state = take(k, [pages, arrived[k]], k + 1, state)

time: 70.1 us -> 70.1 us (level)
  the two profiles are of different devices: /device:TPU:0 before, /device:TPU:5 now
where the time goes in v1:
time: 70.1 us; the launch traced here: 69.2 us
  waiting for transfers between devices  32.1 us (46%)
  Pallas kernels  17.1 us (24%)
  starting transfers between devices  17 us (24%)
  between operations  2.12 us (3%)
  local copies, waits for them, and re-layouts  0.78 us (1%)
    ppermute x7, waiting for transfers between devices, move(): return lax.ppermute(x, ('pool', 'sub'), pairs)  30.6 us
    ppermute x7, starting transfers between devices, move(): return lax.ppermute(x, ('pool', 'sub'), pairs)  16.3 us
    pallas_call x4, Pallas kernels, attend(): pl.pallas_call(functools.partial(attend_kernel, size, k, len(after), len(...  7.3 us
    pallas_call x2, Pallas kernels, pack(): pl.pallas_call(functools.partial(pack_kernel, size, plan, more), out_shap...  5.98 us
    pallas_call x4, Pallas kernels, rebuild(): pl.pallas_call(functools.partial(rebuild_kernel, size, len(high) > 1, sta...  2.17 us
    ppermute x4, waiting for transfers between devices, swapped(): return lax.ppermute(x, 'sub', [(0, 1), (1, 0)])  1.53 us
  transfers between devices with their start and end apart: 11, of which 4 were waited for; matrix products, arithmetic and copies ran while one was open for 0% of the time, Pallas kernels for 19%

profile of v1, /device:TPU:5, one launch (start us, length us, event | category | flops | bytes accessed | tf_op | source)
XLA Modules:
  0.0 69.2 jit_solution(4003298277424258264)
XLA Ops:
  0.6 2.7 %shard_map.89 = bf16[2192,128]{1,0:T(8,128)(2,1)} custom-call(s32[4]{0:T(128)} %route.3, s32[4]{0:T(128)} %lengths.3, bf16[4,2,256,512]{3,2,1,0:T(8,128)(2,1)} %deltas.3, bf16[4,2,16,512]{3,2,1,0:T(8,128)(2,1)} %anchors.3, bf16[4,2,512]{2,1,0:T(2,128)(2,1)} %scale.3), custom_call_target="tpu_custom_call" | custom-call | bytes 524288 | tf_op jit(solution)/shard_map/pallas_call | solution.py:162
  3.3 1.4 %collective-permute-start.8 = (bf16[2192,128]{1,0:T(8,128)(2,1)}, bf16[2192,128]{1,0:T(8,128)(2,1)S(1)}, u32[]{:S(2)}, u32[]{:S(2)}) collective-permute-start(bf16[2192,128]{1,0:T(8,128)(2,1)} %shard_map.89), channel_id=1, source_target_pairs={{0,8},{1,5},{4,12},{5,1},{8,0},{9,13},{12,4},{13,9},{2,10},{3,7},{... | collective-permute-start | bytes 1683464 | tf_op jit(solution)/shard_map/ppermute | solution.py:446
  4.7 3.3 %shard_map.87 = (bf16[2192,128]{1,0:T(8,128)(2,1)}, bf16[1104,128]{1,0:T(8,128)(2,1)S(1)}, bf16[2208,128]{1,0:T(8,128)(2,1)S(1)}, bf16[2192,128]{1,0:T(8,128)(2,...) custom-call(s32[4]{0:T(128)} %route.3, s32[4]{0:T(128)} %lengths.3, ...), custom_call_target="tpu_custom_call" | custom-call | bytes 1572864 | tf_op jit(solution)/shard_map/pallas_call | solution.py:162
  8.0 0.0 copy-start.2
  8.0 0.7 copy-done.2
  8.7 0.0 copy-start.4
  8.7 0.7 collective-permute-start.7
  9.4 0.7 %collective-permute-start.4 = (bf16[2192,128]{1,0:T(8,128)(2,1)}, bf16[2192,128]{1,0:T(8,128)(2,1)S(1)}, u32[]{:S(2)}, u32[]{:S(2)}) collective-permute-start(bf16[2192,128]{1,0:T(8,128)(2,1)} %get-tuple-element.68), channel_id=1, source_target_pairs={{0,12},{4,8},{8,4},{12,0},{2,14},{6,10},{10,6},{14,2},{16,28},{20,... | collective-permute-start | bytes 1683464 | tf_op jit(solution)/shard_map/ppermute | solution.py:446
  10.1 4.2 %collective-permute-start.5 = (s32[8,128]{1,0:T(8,128)S(1)}, s32[8,128]{1,0:T(8,128)S(1)}, u32[]{:S(2)}, u32[]{:S(2)}) collective-permute-start(s32[8,128]{1,0:T(8,128)S(1)} %get-tuple-element.69.refs_0_), channel_id=1, source_target_pairs={{1,9},{5,13},{9,1},{13,5},{3,11},{7,15},{11,3},{15,7},{17,25},{21,... | collective-permute-start | bytes 12296 | tf_op jit(solution)/shard_map/ppermute | solution.py:446
  14.3 1.9 %collective-permute-start.6 = (s32[8,128]{1,0:T(8,128)S(1)}, s32[8,128]{1,0:T(8,128)S(1)}, u32[]{:S(2)}, u32[]{:S(2)}) collective-permute-start(s32[8,128]{1,0:T(8,128)S(1)} %get-tuple-element.70.refs_1_), channel_id=1, source_target_pairs={{1,13},{5,9},{9,5},{13,1},{3,15},{7,11},{11,7},{15,3},{17,29},{21,... | collective-permute-start | bytes 12296 | tf_op jit(solution)/shard_map/ppermute | solution.py:446
  16.2 0.9 %shard_map.86 = (bf16[4,2,32,128]{3,2,1,0:T(8,128)(2,1)S(1)}, bf16[4,2,2,16,128]{4,3,2,1,0:T(8,128)(2,1)S(1)}) custom-call(bf16[4,4,2048]{2,1,0:T(4,128)(2,1)} %new_query.1, bf16[4,2,4,512]{3,2,1,0:T(4,128)(2,1)} %new_kv.1), custom_call_target="tpu_custom_call" | custom-call | tf_op jit(solution)/shard_map/pallas_call | solution.py:226
  17.2 0.0 collective-permute-done.5.refs_2_.refs_1_
  17.2 3.4 %collective-permute-done.6.refs_3_.refs_1_ = s32[8,128]{1,0:T(8,128)S(1)} collective-permute-done((s32[8,128]{1,0:T(8,128)S(1)}, s32[8,128]{1,0:T(8,128)S(1)}, u32[]{:S(2)}, u32[]{:S(2)}) %collective-permute-start.6) | collective-permute-done | bytes 4128 | tf_op jit(solution)/shard_map/ppermute | solution.py:446
  20.6 0.7 %shard_map.88 = (s32[1]{0:T(128)}, s32[1]{0:T(128)}) custom-call(s32[8,128]{1,0:T(8,128)S(1)} %get-tuple-element.69.refs_0_, s32[8,128]{1,0:T(8,128)S(1)} %get-tuple-element.70.refs_1_, s32[8,128]{1,0:T(8,128)S(1)} %collective-permute-done.5.refs_2_.refs_1_, s32[8,128]{1,0:T(8,128)S(1)} %collective-permute-done.6.refs_3_.refs_1_, ...), custom_call_target="tpu_custom_call" | custom-call | tf_op jit(solution)/shard_map/pallas_call | solution.py:197
  22.0 0.0 copy-done.4
  22.0 22.5 %conditional.2 = (bf16[2208,128]{1,0:T(8,128)(2,1)S(1)}) conditional(s32[]{:T(128)} %bitcast.1, bf16[2208,128]{1,0:T(8,128)(2,1)S(1)} %get-tuple-element.76, (bf16[1104,128]{1,0:T(8,128)(2,1)}, bf16[2208,128]{1,0:T(8,128)(2,1)S(1)}) %tuple.34, bf16[2208,128]{1,0:T(8,128)(2,1)S(1)} %get-tuple-element.76), branch_computations={%region_0.0_spmd, %region_1.0_spmd, %region_2.0_spmd} | conditional | flops 1130496 | bytes 3391536 | solution.py:456
  22.0 2.2 %collective-permute-start = (bf16[2208,128]{1,0:T(8,128)(2,1)S(1)}, bf16[2208,128]{1,0:T(8,128)(2,1)S(1)}, u32[]{:S(2)}, u32[]{:S(2)}) collective-permute-start(bf16[2208,128]{1,0:T(8,128)(2,1)S(1)} %param.2), channel_id=1, source_target_pairs={{1,9},{5,13},{9,1},{13,5},{3,11},{7,15},{11,3},{15,7},{17,25},{21,... | collective-permute-start | bytes 1695752 | tf_op jit(solution)/shard_map/cond/branch_2_fun/ppermute | solution.py:446
  24.2 20.2 %collective-permute-done = bf16[2208,128]{1,0:T(8,128)(2,1)S(1)} collective-permute-done((bf16[2208,128]{1,0:T(8,128)(2,1)S(1)}, bf16[2208,128]{1,0:T(8,128)(2,1)S(1)}, u32[]{:S(2)}, u32[]{:S(2)}) %collective-permute-start) | collective-permute-done | bytes 565280 | tf_op jit(solution)/shard_map/cond/branch_2_fun/ppermute | solution.py:446
  44.5 0.0 collective-permute-done.8.low.refs_0_
  44.5 0.9 %shard_map.90 = (bf16[4,2,256,512]{3,2,1,0:T(8,128)(2,1)}, bf16[4,4,2048]{2,1,0:T(4,128)(2,1)}, bf16[1024,128]{1,0:T(8,128)(2,1)S(1)}, bf16[1024,128]{1,0:T(8,128)(2,1)}, f32[8,128]{1,0:T(8,128)S(1)}) custom-call(bf16[2192,128]{1,0:T(8,128)(2,1)S(1)} %collective-permute-done.8.low.refs_0_, bf16[2208,128]{1,0:T(8,128)(2,1)S(1)} %get-tuple-element.106.refs_0_, ...), custom_call_target="tpu_custom_call" | custom-call | flops 1048576 | bytes 1572864 | tf_op jit(solution)/shard_map/pallas_call | solution.py:315
  45.4 0.0 copy-start
  45.4 0.0 collective-permute-done.7.low
  45.4 0.9 %shard_map.91 = (bf16[4,2,256,512]{3,2,1,0:T(8,128)(2,1)}, bf16[4,4,2048]{2,1,0:T(4,128)(2,1)}, bf16[1024,128]{1,0:T(8,128)(2,1)S(1)}, bf16[1024,128]{1,0:T(8,128)(2,1)}, f32[8,128]{1,0:T(8,128)S(1)}) custom-call(bf16[2192,128]{1,0:T(8,128)(2,1)S(1)} %collective-permute-done.7.low, ...), custom_call_target="tpu_custom_call", output_to_operand_aliasing={{0}: (2, {}), {1}: (3, {})} | custom-call | flops 1048576 | bytes 1572864 | tf_op jit(solution)/shard_map/pallas_call | solution.py:315
  46.3 0.0 copy-start.3
  46.3 0.2 shard_map.92
  46.5 0.0 copy-done
  46.5 0.1 collective-permute-start.11
  46.6 0.5 collective-permute-start.10
  47.1 0.1 collective-permute-start.9
  47.8 0.0 copy-done.3
  47.8 12.2 %conditional.3 = (bf16[2208,128]{1,0:T(8,128)(2,1)S(1)}) conditional(s32[]{:T(128)} %bitcast, bf16[2208,128]{1,0:T(8,128)(2,1)S(1)} %get-tuple-element.82, (bf16[1104,128]{1,0:T(8,128)(2,1)S(1)}, bf16[2208,128]{1,0:T(8,128)(2,1)S(1)}) %tuple.33, bf16[2208,128]{1,0:T(8,128)(2,1)S(1)} %get-tuple-element.82), branch_computations={%region_3.0_spmd, %region_4.0_spmd, %region_5.0_spmd} | conditional | flops 1130496 | bytes 3391536 | solution.py:456
  47.8 5.2 %collective-permute-start.1 = (bf16[2208,128]{1,0:T(8,128)(2,1)S(1)}, bf16[2208,128]{1,0:T(8,128)(2,1)S(1)}, u32[]{:S(2)}, u32[]{:S(2)}) collective-permute-start(bf16[2208,128]{1,0:T(8,128)(2,1)S(1)} %param.5), channel_id=1, source_target_pairs={{1,13},{5,9},{9,5},{13,1},{3,15},{7,11},{11,7},{15,3},{17,29},{21,... | collective-permute-start | bytes 1695752 | tf_op jit(solution)/shard_map/cond/branch_2_fun/ppermute | solution.py:446
  53.0 7.0 %collective-permute-done.1 = bf16[2208,128]{1,0:T(8,128)(2,1)S(1)} collective-permute-done((bf16[2208,128]{1,0:T(8,128)(2,1)S(1)}, bf16[2208,128]{1,0:T(8,128)(2,1)S(1)}, u32[]{:S(2)}, u32[]{:S(2)}) %collective-permute-start.1) | collective-permute-done | bytes 565280 | tf_op jit(solution)/shard_map/cond/branch_2_fun/ppermute | solution.py:446
  60.0 0.0 collective-permute-done.11.other
  60.0 1.3 %shard_map.93 = (bf16[4,2,256,512]{3,2,1,0:T(8,128)(2,1)}, bf16[4,4,2048]{2,1,0:T(4,128)(2,1)}) custom-call(bf16[4,2,32,128]{3,2,1,0:T(8,128)(2,1)S(1)} %get-tuple-element.66.query, bf16[4,2,2,16,128]{4,3,2,1,0:T(8,128)(2,1)S(1)} %get-tuple-element.67.refs_4_.new_kv, ...), custom_call_target="tpu_custom_call", output_to_operand_aliasing={{0}: (7, {}), {1}: (8, {})} | custom-call | flops 16777216 | bytes 1048576 | tf_op jit(solution)/shard_map/pallas_call | solution.py:410
  61.4 0.0 copy-start.1
  61.4 0.0 collective-permute-done.10.other
  61.4 2.3 %shard_map.94 = (bf16[4,2,256,512]{3,2,1,0:T(8,128)(2,1)}, bf16[4,4,2048]{2,1,0:T(4,128)(2,1)}) custom-call(bf16[4,2,32,128]{3,2,1,0:T(8,128)(2,1)S(1)} %get-tuple-element.66.query, bf16[4,2,2,16,128]{4,3,2,1,0:T(8,128)(2,1)S(1)} %get-tuple-element.67.refs_4_.new_kv, ...), custom_call_target="tpu_custom_call", output_to_operand_aliasing={{0}: (7, {}), {1}: (8, {})} | custom-call | flops 16777216 | bytes 1048576 | tf_op jit(solution)/shard_map/pallas_call | solution.py:410
  63.8 0.0 collective-permute-done.9.other
  63.8 0.0 copy-done.1
  63.8 2.3 %shard_map.95 = (bf16[4,2,256,512]{3,2,1,0:T(8,128)(2,1)}, bf16[4,4,2048]{2,1,0:T(4,128)(2,1)}) custom-call(bf16[4,2,32,128]{3,2,1,0:T(8,128)(2,1)S(1)} %get-tuple-element.66.query, bf16[4,2,2,16,128]{4,3,2,1,0:T(8,128)(2,1)S(1)} %get-tuple-element.67.refs_4_.new_kv, ...), custom_call_target="tpu_custom_call", output_to_operand_aliasing={{0}: (7, {}), {1}: (8, {})} | custom-call | flops 16777216 | bytes 1048576 | tf_op jit(solution)/shard_map/pallas_call | solution.py:410
  66.1 0.0 collective-permute-done.4.low
  66.1 0.2 shard_map.96
  66.3 0.1 collective-permute-start.12
  66.4 1.5 %collective-permute-done.12.other = bf16[1024,128]{1,0:T(8,128)(2,1)S(1)} collective-permute-done((bf16[1024,128]{1,0:T(8,128)(2,1)S(1)}, bf16[1024,128]{1,0:T(8,128)(2,1)S(1)}, u32[]{:S(2)}, u32[]{:S(2)}) %collective-permute-start.12) | collective-permute-done | bytes 262176 | tf_op jit(solution)/shard_map/ppermute | solution.py:459
  67.9 1.3 %shard_map.97 = (bf16[4,2,256,512]{3,2,1,0:T(8,128)(2,1)}, bf16[4,4,2048]{2,1,0:T(4,128)(2,1)}) custom-call(bf16[4,2,32,128]{3,2,1,0:T(8,128)(2,1)S(1)} %get-tuple-element.66.query, bf16[4,2,2,16,128]{4,3,2,1,0:T(8,128)(2,1)S(1)} %get-tuple-element.67.refs_4_.new_kv, ...), custom_call_target="tpu_custom_call", output_to_operand_aliasing={{0}: (6, {}), {1}: (7, {})} | custom-call | flops 16777216 | bytes 1048576 | tf_op jit(solution)/shard_map/pallas_call | solution.py:410
  (2 shorter events, 0.1 us)
Async XLA Ops:
  3.3 41.2 %collective-permute-start.8 = (bf16[2192,128]{1,0:T(8,128)(2,1)}, bf16[2192,128]{1,0:T(8,128)(2,1)S(1)}, u32[]{:S(2)}, u32[]{:S(2)}) collective-permute-start(bf16[2192,128]{1,0:T(8,128)(2,1)} %shard_map.89), channel_id=1, source_target_pairs={{0,8},{1,5},{4,12},{5,1},{8,0},{9,13},{12,4},{13,9},{2,10},{3,7},{... | collective-permute-start | bytes 1683464 | tf_op jit(solution)/shard_map/ppermute | solution.py:446
  8.0 0.7 %copy-start.2 = (bf16[1104,128]{1,0:T(8,128)(2,1)}, bf16[1104,128]{1,0:T(8,128)(2,1)S(1)}, u32[]{:S(2)}) copy-start(bf16[1104,128]{1,0:T(8,128)(2,1)S(1)} %get-tuple-element.83) | copy-start | bytes 847876
  8.7 13.3 %copy-start.4 = (bf16[1104,128]{1,0:T(8,128)(2,1)}, bf16[1104,128]{1,0:T(8,128)(2,1)S(1)}, u32[]{:S(2)}) copy-start(bf16[1104,128]{1,0:T(8,128)(2,1)S(1)} %get-tuple-element.77) | copy-start | bytes 847876
  8.7 36.7 %collective-permute-start.7 = (bf16[2192,128]{1,0:T(8,128)(2,1)}, bf16[2192,128]{1,0:T(8,128)(2,1)S(1)}, u32[]{:S(2)}, u32[]{:S(2)}) collective-permute-start(bf16[2192,128]{1,0:T(8,128)(2,1)} %get-tuple-element.74), channel_id=1, source_target_pairs={{0,4},{4,0},{8,12},{12,8},{2,6},{6,2},{10,14},{14,10},{16,20},{20,... | collective-permute-start | bytes 1683464 | tf_op jit(solution)/shard_map/ppermute | solution.py:446
  9.4 56.7 %collective-permute-start.4 = (bf16[2192,128]{1,0:T(8,128)(2,1)}, bf16[2192,128]{1,0:T(8,128)(2,1)S(1)}, u32[]{:S(2)}, u32[]{:S(2)}) collective-permute-start(bf16[2192,128]{1,0:T(8,128)(2,1)} %get-tuple-element.68), channel_id=1, source_target_pairs={{0,12},{4,8},{8,4},{12,0},{2,14},{6,10},{10,6},{14,2},{16,28},{20,... | collective-permute-start | bytes 1683464 | tf_op jit(solution)/shard_map/ppermute | solution.py:446
  10.1 7.1 %collective-permute-start.5 = (s32[8,128]{1,0:T(8,128)S(1)}, s32[8,128]{1,0:T(8,128)S(1)}, u32[]{:S(2)}, u32[]{:S(2)}) collective-permute-start(s32[8,128]{1,0:T(8,128)S(1)} %get-tuple-element.69.refs_0_), channel_id=1, source_target_pairs={{1,9},{5,13},{9,1},{13,5},{3,11},{7,15},{11,3},{15,7},{17,25},{21,... | collective-permute-start | bytes 12296 | tf_op jit(solution)/shard_map/ppermute | solution.py:446
  14.3 6.3 %collective-permute-start.6 = (s32[8,128]{1,0:T(8,128)S(1)}, s32[8,128]{1,0:T(8,128)S(1)}, u32[]{:S(2)}, u32[]{:S(2)}) collective-permute-start(s32[8,128]{1,0:T(8,128)S(1)} %get-tuple-element.70.refs_1_), channel_id=1, source_target_pairs={{1,13},{5,9},{9,5},{13,1},{3,15},{7,11},{11,7},{15,3},{17,29},{21,... | collective-permute-start | bytes 12296 | tf_op jit(solution)/shard_map/ppermute | solution.py:446
  22.0 22.5 %collective-permute-start = (bf16[2208,128]{1,0:T(8,128)(2,1)S(1)}, bf16[2208,128]{1,0:T(8,128)(2,1)S(1)}, u32[]{:S(2)}, u32[]{:S(2)}) collective-permute-start(bf16[2208,128]{1,0:T(8,128)(2,1)S(1)} %param.2), channel_id=1, source_target_pairs={{1,9},{5,13},{9,1},{13,5},{3,11},{7,15},{11,3},{15,7},{17,25},{21,... | collective-permute-start | bytes 1695752 | tf_op jit(solution)/shard_map/cond/branch_2_fun/ppermute | solution.py:446
  45.4 1.1 %copy-start = (bf16[1024,128]{1,0:T(8,128)(2,1)}, bf16[1024,128]{1,0:T(8,128)(2,1)S(1)}, u32[]{:S(2)}) copy-start(bf16[1024,128]{1,0:T(8,128)(2,1)S(1)} %get-tuple-element.85.mine) | copy-start | bytes 786436
  46.3 1.5 %copy-start.3 = (bf16[1104,128]{1,0:T(8,128)(2,1)S(1)}, bf16[1104,128]{1,0:T(8,128)(2,1)}, u32[]{:S(2)}) copy-start(bf16[1104,128]{1,0:T(8,128)(2,1)} %copy-done.2) | copy-start | bytes 847876
  46.5 13.5 %collective-permute-start.11 = (bf16[1024,128]{1,0:T(8,128)(2,1)S(1)}, bf16[1024,128]{1,0:T(8,128)(2,1)S(1)}, u32[]{:S(2)}, u32[]{:S(2)}) collective-permute-start(bf16[1024,128]{1,0:T(8,128)(2,1)S(1)} %get-tuple-element.92.theirs), channel_id=1, source_target_pairs={{0,1},{1,0},{2,3},{3,2},{4,5},{5,4},{6,7},{7,6},{8,9},{9,8},{10,11... | collective-permute-start | bytes 786440 | tf_op jit(solution)/shard_map/ppermute | solution.py:459
  46.6 14.8 %collective-permute-start.10 = (bf16[1024,128]{1,0:T(8,128)(2,1)}, bf16[1024,128]{1,0:T(8,128)(2,1)S(1)}, u32[]{:S(2)}, u32[]{:S(2)}) collective-permute-start(bf16[1024,128]{1,0:T(8,128)(2,1)} %get-tuple-element.89.theirs), channel_id=1, source_target_pairs={{0,1},{1,0},{2,3},{3,2},{4,5},{5,4},{6,7},{7,6},{8,9},{9,8},{10,11... | collective-permute-start | bytes 786440 | tf_op jit(solution)/shard_map/ppermute | solution.py:459
  47.1 16.7 %collective-permute-start.9 = (bf16[1024,128]{1,0:T(8,128)(2,1)}, bf16[1024,128]{1,0:T(8,128)(2,1)S(1)}, u32[]{:S(2)}, u32[]{:S(2)}) collective-permute-start(bf16[1024,128]{1,0:T(8,128)(2,1)} %get-tuple-element.86.theirs), channel_id=1, source_target_pairs={{0,1},{1,0},{2,3},{3,2},{4,5},{5,4},{6,7},{7,6},{8,9},{9,8},{10,11... | collective-permute-start | bytes 786440 | tf_op jit(solution)/shard_map/ppermute | solution.py:459
  47.8 12.2 %collective-permute-start.1 = (bf16[2208,128]{1,0:T(8,128)(2,1)S(1)}, bf16[2208,128]{1,0:T(8,128)(2,1)S(1)}, u32[]{:S(2)}, u32[]{:S(2)}) collective-permute-start(bf16[2208,128]{1,0:T(8,128)(2,1)S(1)} %param.5), channel_id=1, source_target_pairs={{1,13},{5,9},{9,5},{13,1},{3,15},{7,11},{11,7},{15,3},{17,29},{21,... | collective-permute-start | bytes 1695752 | tf_op jit(solution)/shard_map/cond/branch_2_fun/ppermute | solution.py:446
  61.4 2.4 %copy-start.1 = (bf16[1024,128]{1,0:T(8,128)(2,1)S(1)}, bf16[1024,128]{1,0:T(8,128)(2,1)}, u32[]{:S(2)}) copy-start(bf16[1024,128]{1,0:T(8,128)(2,1)} %copy-done) | copy-start | bytes 786436
  66.3 1.6 %collective-permute-start.12 = (bf16[1024,128]{1,0:T(8,128)(2,1)S(1)}, bf16[1024,128]{1,0:T(8,128)(2,1)S(1)}, u32[]{:S(2)}, u32[]{:S(2)}) collective-permute-start(bf16[1024,128]{1,0:T(8,128)(2,1)S(1)} %get-tuple-element.103.theirs), channel_id=1, source_target_pairs={{0,1},{1,0},{2,3},{3,2},{4,5},{5,4},{6,7},{7,6},{8,9},{9,8},{10,11... | collective-permute-start | bytes 786440 | tf_op jit(solution)/shard_map/ppermute | solution.py:459
